TPU v7x, 32 devices: a whole 2x2x4 slice. The times are simulated.
32 devices in a mesh: tm: 2 (over core), tile: 8 (over z, x), sect: 2 (over y).
Axes of the slice: x: 2, y: 2, z: 4, core: 2. Of those that a mesh axis runs over, the one named last changes fastest.
Arguments:
- latents: bfloat16 [2, 8, 8, 8, 4, 16], P(None, ('tm', 'sect'), 'tile'), may hold values from -400 to 400
- in_weight: bfloat16 [3, 3, 3, 16, 512], replicated, may hold values from -0.3125 to 0.3125
- gn_gain: float32 [512], replicated, may hold values from 0.1 to 1.9
- gn_shift: float32 [512], replicated, may hold values from -3 to 3
- up_weight: bfloat16 [3, 3, 3, 512, 256], replicated, may hold values from -0.0546875 to 0.0546875
Outputs:
- decoded: bfloat16 [2, 8, 8, 16, 8, 256], P('sect', 'tm', 'tile')
All inputs are finite; a program needn't handle non-finite values.
Results may differ from a plain program's by a relative error of at most 0.005.
Values may be sent and summed in bfloat16 or wider, within the bound.
A program may use at most 64 MiB of HBM per device.

v0:
```python
import jax
import jax.numpy as jnp
from jax import lax
from jax.sharding import PartitionSpec as P

GROUPS = 32


EPSILON = 1e-06


def padded_2(value, sides, width):
    for axis, dim in sides:
        size, length = (lax.axis_size(axis), value.shape[dim])
        up = [(i, (i + 1) % size) for i in range(size - 1)]
        down = [(j, i) for i, j in up]
        last = lax.slice_in_dim(value, length - width, length, axis=dim)
        first = lax.slice_in_dim(value, 0, width, axis=dim)
        before = lax.ppermute(last, axis, up)
        after = lax.ppermute(first, axis, down)
        value = jnp.concatenate([before, value, after], axis=dim)
    return value


def shifted(value, axis, by):
    size = lax.axis_size(axis)
    pairs = [(i, i + by) for i in range(size) if 0 <= i + by < size]
    return lax.ppermute(value, axis, pairs)


def width_stack(padded):
    inner_cols = padded.shape[-2] - 2
    return jnp.concatenate(
        [
            padded[..., 0:inner_cols, :],
            padded[..., 1 : inner_cols + 1, :],
            padded[..., 2 : inner_cols + 2, :],
        ],
        axis=-1,
    )


def causal_conv(padded, weight):
    stacked = width_stack(padded)
    batch_len, frames_in, rows_in, inner_cols, merged = stacked.shape
    out_frames = frames_in - 2
    out_rows = rows_in - 2
    out_chans = weight.shape[-1]
    kernel = weight.reshape(3, 3, merged, out_chans)
    accum_sum = jnp.zeros((batch_len * out_frames * out_rows * inner_cols, out_chans), jnp.float32)
    for tap_t in range(3):
        for tap_h in range(3):
            tap_rows = stacked[:, tap_t : tap_t + out_frames, tap_h : tap_h + out_rows].reshape(
                -1, merged
            )
            accum_sum = accum_sum + jnp.dot(
                tap_rows, kernel[tap_t, tap_h], preferred_element_type=jnp.float32
            )
    return accum_sum.reshape(batch_len, out_frames, out_rows, inner_cols, out_chans)


def upsample_twice(values):
    in_shape = values.shape
    leading = in_shape[:-3]
    rows_in, cols_in, chans = (in_shape[-3], in_shape[-2], in_shape[-1])
    grown = jnp.broadcast_to(
        values[..., :, None, :, None, :], leading + (rows_in, 2, cols_in, 2, chans)
    )
    return grown.reshape(leading + (2 * rows_in, 2 * cols_in, chans))


def apply_norm(pre, group_mean, inv_std, gn_gain, gn_shift, groups):
    in_shape = pre.shape
    grouped = pre.reshape(in_shape[:-1] + (groups, in_shape[-1] // groups))
    lead_ones = (1,) * (len(in_shape) - 2)
    center = group_mean.reshape((in_shape[0],) + lead_ones + (groups, 1))
    spread = inv_std.reshape((in_shape[0],) + lead_ones + (groups, 1))
    normed = ((grouped - center) * spread).reshape(in_shape)
    return jax.nn.silu(normed * gn_gain + gn_shift).astype(jnp.bfloat16)


def column_keep(cols_in, depth, col_idx, col_count):
    col_ids = jnp.arange(cols_in + 2 * depth)
    keep = ((col_ids >= depth) | (col_idx > 0)) & (
        (col_ids < cols_in + depth) | (col_idx < col_count - 1)
    )
    return keep[None, None, None, :, None]


def latent_margin(values, depth, col_idx, col_count):
    tile_cols = values.shape[3]
    sided = padded_2(values, (("tile", 3),), depth)
    sided = jnp.where(
        column_keep(tile_cols, depth, col_idx, col_count), sided, jnp.zeros((), sided.dtype)
    )
    return jnp.pad(sided, ((0, 0), (0, 0), (depth, depth), (0, 0), (0, 0)))


def act_margin(values, col_idx, col_count):
    tile_cols = values.shape[3]
    sided = padded_2(values, (("tile", 3),), 1)
    sided = jnp.where(
        column_keep(tile_cols, 1, col_idx, col_count), sided, jnp.zeros((), sided.dtype)
    )
    return jnp.pad(sided, ((0, 0), (0, 0), (1, 1), (0, 0), (0, 0)))


def shards(latents, in_weight, gn_gain, gn_shift, up_weight):
    lat_local = lax.all_to_all(latents, "sect", split_axis=0, concat_axis=1, tiled=True)[:, :, 0]
    clip_dev, span_len, tile_rows, tile_cols, lat_chans = lat_local.shape
    chans = in_weight.shape[-1]
    group_size = chans // GROUPS
    col_idx = lax.axis_index("tile")
    col_count = lax.axis_size("tile")
    cell_count = span_len * lax.axis_size("tm") * tile_rows * tile_cols * col_count * group_size
    lat_ext = latent_margin(lat_local, 1, col_idx, col_count)
    earlier = shifted(lat_ext[:, span_len - 2 :], "tm", 1)
    pre_own = causal_conv(jnp.concatenate([earlier, lat_ext], axis=1), in_weight)
    grouped = pre_own.reshape(clip_dev, -1, GROUPS, group_size)
    group_mean = lax.psum(jnp.sum(grouped, axis=(1, 3)), ("tm", "tile")) / cell_count
    centered = jnp.sum(jnp.square(grouped - group_mean[:, None, :, None]), axis=(1, 3))
    group_var = lax.psum(centered, ("tm", "tile")) / cell_count
    inv_std = lax.rsqrt(group_var + EPSILON)
    act_own = apply_norm(pre_own, group_mean, inv_std, gn_gain, gn_shift, GROUPS)
    act_ext = act_margin(act_own, col_idx, col_count)
    act_prev = shifted(act_ext[:, span_len - 2 :], "tm", 1)
    padded_act = jnp.concatenate([act_prev, act_ext], axis=1)
    grown = upsample_twice(padded_act)[:, :, 1 : 2 * tile_rows + 3, 1 : 2 * tile_cols + 3]
    return causal_conv(grown, up_weight).astype(jnp.bfloat16)[:, :, None]


def solution(mesh):
    placed = (P(None, ("tm", "sect"), "tile", None, None, None), P(), P(), P(), P())
    return jax.shard_map(
        shards,
        mesh=mesh,
        in_specs=placed,
        out_specs=P("sect", "tm", "tile", None, None, None),
        check_vma=False,
    )
```

profile of v0, /device:TPU:0, one launch (start us, length us, event | category | flops | bytes accessed | tf_op | source)
XLA Modules:
  0.0 119.7 jit_solution(10080181706625635830)
XLA Ops:
  0.0 1.5 %reshape.286 = bf16[2,2,512]{2,1,0:T(2,128)(2,1)} reshape(bf16[2,2,1,8,4,16]{5,4,3,2,1,0:T(4,128)(2,1)} %param.5) | data formatting | bytes 8192
  1.5 4.2 %all-to-all-start = ((bf16[2,2,512]{2,1,0:T(2,128)(2,1)}), bf16[2,2,512]{2,1,0:T(2,128)(2,1)S(1)}, u32[]{:S(2)}, u32[]{:S(2)}) async-start(bf16[2,2,512]{2,1,0:T(2,128)(2,1)} %reshape.286), calls=%async_computation | async-start | bytes 8192 | tf_op jit(solution)/shard_map/all_to_all | solution.py:109
  5.7 3.8 %all-to-all-done = bf16[2,2,512]{2,1,0:T(2,128)(2,1)S(1)} async-done(((bf16[2,2,512]{2,1,0:T(2,128)(2,1)}), bf16[2,2,512]{2,1,0:T(2,128)(2,1)S(1)}, u32[]{:S(2)}, u32[]{:S(2)}) %all-to-all-start) | async-done | bytes 4128 | tf_op jit(solution)/shard_map/all_to_all | solution.py:109
  9.7 3.8 %collective-permute-start = (bf16[1,4,8,1,16]{4,3,2,1,0:T(2,128)(2,1)S(1)}, bf16[1,4,8,1,16]{4,3,2,1,0:T(2,128)(2,1)S(1)}, u32[]{:S(2)}, u32[]{:S(2)}) collective-permute-start(bf16[1,4,8,1,16]{4,3,2,1,0:T(2,128)(2,1)S(1)} %get-tuple-element.30), channel_id=1, source_target_pairs={{0,2},{2,4},{4,6},{6,8},{8,10},{10,12},{12,14},{1,3},{3,5},{5,7},{... | collective-permute-start | bytes 3080 | tf_op jit(solution)/shard_map/ppermute | solution.py:19
  13.5 1.3 %collective-permute-start.1 = (bf16[1,4,8,1,16]{4,3,2,1,0:T(2,128)(2,1)S(1)}, bf16[1,4,8,1,16]{4,3,2,1,0:T(2,128)(2,1)S(1)}, u32[]{:S(2)}, u32[]{:S(2)}) collective-permute-start(bf16[1,4,8,1,16]{4,3,2,1,0:T(2,128)(2,1)S(1)} %get-tuple-element.31), channel_id=1, source_target_pairs={{2,0},{4,2},{6,4},{8,6},{10,8},{12,10},{14,12},{3,1},{5,3},{7,5},{... | collective-permute-start | bytes 3080 | tf_op jit(solution)/shard_map/ppermute | solution.py:20
  14.9 4.2 %collective-permute-done.1 = bf16[1,4,8,1,16]{4,3,2,1,0:T(2,128)(2,1)S(1)} collective-permute-done((bf16[1,4,8,1,16]{4,3,2,1,0:T(2,128)(2,1)S(1)}, bf16[1,4,8,1,16]{4,3,2,1,0:T(2,128)(2,1)S(1)}, u32[]{:S(2)}, u32[]{:S(2)}) %collective-permute-start.1) | collective-permute-done | bytes 1056 | tf_op jit(solution)/shard_map/ppermute | solution.py:20
  19.2 1.3 %collective-permute-start.2 = (bf16[1,2,10,6,16]{4,3,2,1,0:T(8,128)(2,1)S(1)}, bf16[1,2,10,6,16]{4,3,2,1,0:T(8,128)(2,1)S(1)}, u32[]{:S(2)}, u32[]{:S(2)}) collective-permute-start(bf16[1,2,10,6,16]{4,3,2,1,0:T(8,128)(2,1)S(1)} %pad_slice_fusion.4), channel_id=1, source_target_pairs={{0,16},{1,17},{2,18},{3,19},{4,20},{5,21},{6,22},{7,23},{8,24},{9,... | collective-permute-start | bytes 11528 | tf_op jit(solution)/shard_map/ppermute | solution.py:28
  23.7 32.4 %psum.14 = f32[1,32]{1,0:T(1,128)S(1)} all-reduce(f32[1,32]{1,0:T(1,128)S(1)} %bitcast.151), channel_id=1, replica_groups=mesh['tm'=2,'tile'=8,'sect'=2] {'tm','tile'}, use_global_device_ids=true, to_apply=%region_2.3 | all-reduce | flops 32 | bytes 256 | tf_op jit(solution)/shard_map/psum | solution.py:120
  56.5 29.6 %psum.15 = f32[1,32]{1,0:T(1,128)S(1)} all-reduce(f32[1,32]{1,0:T(1,128)S(1)} %bitcast.150), channel_id=1, replica_groups=mesh['tm'=2,'tile'=8,'sect'=2] {'tm','tile'}, use_global_device_ids=true, to_apply=%region_5.6 | all-reduce | flops 32 | bytes 256 | tf_op jit(solution)/shard_map/psum | solution.py:122
  86.5 4.2 %collective-permute-start.3 = (bf16[1,4,8,1,512]{4,3,2,1,0:T(2,128)(2,1)S(1)}, bf16[1,4,8,1,512]{4,3,2,1,0:T(2,128)(2,1)S(1)}, u32[]{:S(2)}, u32[]{:S(2)}) collective-permute-start(bf16[1,4,8,1,512]{4,3,2,1,0:T(2,128)(2,1)S(1)} %get-tuple-element.17), channel_id=1, source_target_pairs={{0,2},{2,4},{4,6},{6,8},{8,10},{10,12},{12,14},{1,3},{3,5},{5,7},{... | collective-permute-start | bytes 98312 | tf_op jit(solution)/shard_map/ppermute | solution.py:19
  90.7 1.3 %collective-permute-start.4 = (bf16[1,4,8,1,512]{4,3,2,1,0:T(2,128)(2,1)S(1)}, bf16[1,4,8,1,512]{4,3,2,1,0:T(2,128)(2,1)S(1)}, u32[]{:S(2)}, u32[]{:S(2)}) collective-permute-start(bf16[1,4,8,1,512]{4,3,2,1,0:T(2,128)(2,1)S(1)} %get-tuple-element.18), channel_id=1, source_target_pairs={{2,0},{4,2},{6,4},{8,6},{10,8},{12,10},{14,12},{3,1},{5,3},{7,5},{... | collective-permute-start | bytes 98312 | tf_op jit(solution)/shard_map/ppermute | solution.py:20
  92.6 4.3 %collective-permute-done.4 = bf16[1,4,8,1,512]{4,3,2,1,0:T(2,128)(2,1)S(1)} collective-permute-done((bf16[1,4,8,1,512]{4,3,2,1,0:T(2,128)(2,1)S(1)}, bf16[1,4,8,1,512]{4,3,2,1,0:T(2,128)(2,1)S(1)}, u32[]{:S(2)}, u32[]{:S(2)}) %collective-permute-start.4) | collective-permute-done | bytes 32800 | tf_op jit(solution)/shard_map/ppermute | solution.py:20
  97.2 1.3 %collective-permute-start.5 = (bf16[1,2,10,6,512]{4,3,2,1,0:T(8,128)(2,1)S(1)}, bf16[1,2,10,6,512]{4,3,2,1,0:T(8,128)(2,1)S(1)}, u32[]{:S(2)}, u32[]{:S(2)}) collective-permute-start(bf16[1,2,10,6,512]{4,3,2,1,0:T(8,128)(2,1)S(1)} %pad_slice_fusion.5), channel_id=1, source_target_pairs={{0,16},{1,17},{2,18},{3,19},{4,20},{5,21},{6,22},{7,23},{8,24},{9,... | collective-permute-start | bytes 368648 | tf_op jit(solution)/shard_map/ppermute | solution.py:28
  98.5 0.9 collective-permute-done.5
  102.2 3.6 %fusion.9 = (bf16[1,4,16,8,1536]{4,2,3,1,0:T(8,128)(2,1)S(1)}, bf16[1,4,16,8,1536]{4,2,3,1,0:T(8,128)(2,1)S(1)}, bf16[1,4,16,8,1536]{4,2,3,1,0:T(8,128)(2,1)S(1)...) fusion(bf16[1,6,18,8,1536]{4,2,3,1,0:T(8,128)(2,1)S(1)} %pad_ma, ...), kind=kLoop, calls=%fused_computation.60 | loop fusion | bytes 28311552 | tf_op jit(solution)/shard_map/slice | solution.py:53
  105.9 0.9 copy.18
  106.7 0.9 copy.17
  107.6 0.9 copy.16
  108.5 0.9 copy.15
  109.4 0.9 copy.14
  110.3 0.9 copy.13
  111.1 0.9 copy.12
  112.0 0.9 copy.11
  118.4 1.3 %fusion = bf16[512,256]{1,0:T(8,128)(2,1)} fusion(f32[512,256]{1,0:T(8,128)S(1)} %convolution_add_fusion.1, bf16[512,1536]{1,0:T(8,128)(2,1)S(1)} %bitcast.128, bf16[3,3,1536,256]{3,2,1,0:T(8,128)(2,1)S(1)} %bitcast.127), kind=kOutput, calls=%fused_computation.9 | convolution fusion | flops 402915328 | bytes 3145728 | tf_op jit(solution)/shard_map/dot_general | solution.py:56
  (66 shorter events, 13.3 us)
Async XLA Ops:
  0.0 21.7 %copy-start = (bf16[3,3,3,16,512]{4,3,2,1,0:T(8,128)(2,1)S(1)}, bf16[3,3,3,16,512]{4,3,2,1,0:T(8,128)(2,1)}, u32[]{:S(2)}) copy-start(bf16[3,3,3,16,512]{4,3,2,1,0:T(8,128)(2,1)} %param.6) | copy-start | bytes 1327108
  1.5 8.0 %all-to-all-start = ((bf16[2,2,512]{2,1,0:T(2,128)(2,1)}), bf16[2,2,512]{2,1,0:T(2,128)(2,1)S(1)}, u32[]{:S(2)}, u32[]{:S(2)}) async-start(bf16[2,2,512]{2,1,0:T(2,128)(2,1)} %reshape.286), calls=%async_computation | async-start | bytes 8192 | tf_op jit(solution)/shard_map/all_to_all | solution.py:109
  9.7 5.3 %collective-permute-start = (bf16[1,4,8,1,16]{4,3,2,1,0:T(2,128)(2,1)S(1)}, bf16[1,4,8,1,16]{4,3,2,1,0:T(2,128)(2,1)S(1)}, u32[]{:S(2)}, u32[]{:S(2)}) collective-permute-start(bf16[1,4,8,1,16]{4,3,2,1,0:T(2,128)(2,1)S(1)} %get-tuple-element.30), channel_id=1, source_target_pairs={{0,2},{2,4},{4,6},{6,8},{8,10},{10,12},{12,14},{1,3},{3,5},{5,7},{... | collective-permute-start | bytes 3080 | tf_op jit(solution)/shard_map/ppermute | solution.py:19
  13.5 5.6 %collective-permute-start.1 = (bf16[1,4,8,1,16]{4,3,2,1,0:T(2,128)(2,1)S(1)}, bf16[1,4,8,1,16]{4,3,2,1,0:T(2,128)(2,1)S(1)}, u32[]{:S(2)}, u32[]{:S(2)}) collective-permute-start(bf16[1,4,8,1,16]{4,3,2,1,0:T(2,128)(2,1)S(1)} %get-tuple-element.31), channel_id=1, source_target_pairs={{2,0},{4,2},{6,4},{8,6},{10,8},{12,10},{14,12},{3,1},{5,3},{7,5},{... | collective-permute-start | bytes 3080 | tf_op jit(solution)/shard_map/ppermute | solution.py:20
  19.2 2.2 %collective-permute-start.2 = (bf16[1,2,10,6,16]{4,3,2,1,0:T(8,128)(2,1)S(1)}, bf16[1,2,10,6,16]{4,3,2,1,0:T(8,128)(2,1)S(1)}, u32[]{:S(2)}, u32[]{:S(2)}) collective-permute-start(bf16[1,2,10,6,16]{4,3,2,1,0:T(8,128)(2,1)S(1)} %pad_slice_fusion.4), channel_id=1, source_target_pairs={{0,16},{1,17},{2,18},{3,19},{4,20},{5,21},{6,22},{7,23},{8,24},{9,... | collective-permute-start | bytes 11528 | tf_op jit(solution)/shard_map/ppermute | solution.py:28
  22.8 63.5 %copy-start.1 = (f32[512]{0:T(512)S(1)}, f32[512]{0:T(512)}, u32[]{:S(2)}) copy-start(f32[512]{0:T(512)} %param.8) | copy-start | bytes 6148
  22.8 63.5 %copy-start.2 = (f32[512]{0:T(512)S(1)}, f32[512]{0:T(512)}, u32[]{:S(2)}) copy-start(f32[512]{0:T(512)} %param.7) | copy-start | bytes 6148
  86.5 6.1 %collective-permute-start.3 = (bf16[1,4,8,1,512]{4,3,2,1,0:T(2,128)(2,1)S(1)}, bf16[1,4,8,1,512]{4,3,2,1,0:T(2,128)(2,1)S(1)}, u32[]{:S(2)}, u32[]{:S(2)}) collective-permute-start(bf16[1,4,8,1,512]{4,3,2,1,0:T(2,128)(2,1)S(1)} %get-tuple-element.17), channel_id=1, source_target_pairs={{0,2},{2,4},{4,6},{6,8},{8,10},{10,12},{12,14},{1,3},{3,5},{5,7},{... | collective-permute-start | bytes 98312 | tf_op jit(solution)/shard_map/ppermute | solution.py:19
  90.7 6.2 %collective-permute-start.4 = (bf16[1,4,8,1,512]{4,3,2,1,0:T(2,128)(2,1)S(1)}, bf16[1,4,8,1,512]{4,3,2,1,0:T(2,128)(2,1)S(1)}, u32[]{:S(2)}, u32[]{:S(2)}) collective-permute-start(bf16[1,4,8,1,512]{4,3,2,1,0:T(2,128)(2,1)S(1)} %get-tuple-element.18), channel_id=1, source_target_pairs={{2,0},{4,2},{6,4},{8,6},{10,8},{12,10},{14,12},{3,1},{5,3},{7,5},{... | collective-permute-start | bytes 98312 | tf_op jit(solution)/shard_map/ppermute | solution.py:20
  97.2 2.3 %collective-permute-start.5 = (bf16[1,2,10,6,512]{4,3,2,1,0:T(8,128)(2,1)S(1)}, bf16[1,2,10,6,512]{4,3,2,1,0:T(8,128)(2,1)S(1)}, u32[]{:S(2)}, u32[]{:S(2)}) collective-permute-start(bf16[1,2,10,6,512]{4,3,2,1,0:T(8,128)(2,1)S(1)} %pad_slice_fusion.5), channel_id=1, source_target_pairs={{0,16},{1,17},{2,18},{3,19},{4,20},{5,21},{6,22},{7,23},{8,24},{9,... | collective-permute-start | bytes 368648 | tf_op jit(solution)/shard_map/ppermute | solution.py:28
  109.4 4.4 %slice-start = ((s8[7077888]{0:T(1024)(128)(4,1)}), s8[4194304]{0:T(1024)(128)(4,1)S(1)}, s32[]{:S(2)}) async-start(s8[7077888]{0:T(1024)(128)(4,1)} %bitcast.117), calls=%async_computation.1 | async-start | bytes 8388608
  111.1 2.7 %slice-start.1 = ((s8[7077888]{0:T(1024)(128)(4,1)}), s8[2883584]{0:T(1024)(128)(4,1)S(1)}, s32[]{:S(2)}) async-start(s8[7077888]{0:T(1024)(128)(4,1)} %bitcast.117), calls=%async_computation.2 | async-start | bytes 5767168
where the time goes:
time: 120 us
  blocking collectives  62 us (52%)
  starting transfers between devices  17.4 us (14%)
  local copies, waits for them, and re-layouts  16.2 us (14%)
  waiting for transfers between devices  14.5 us (12%)
  matrix products  7.32 us (6%)
  other arithmetic  1.74 us (1%)
    psum x1, blocking collectives, shards(): lax.psum(jnp.sum(grouped, axis=(1, 3)), ('tm', 'tile')) / cell_count  32.4 us
    psum x1, blocking collectives, shards(): group_var = lax.psum(centered, ('tm', 'tile')) / cell_count  29.6 us
    slice x11, local copies, waits for them, and re-layouts, causal_conv(): stacked[:, tap_t:tap_t + out_frames, tap_h:tap_h + out_rows]  11.5 us
    ppermute x2, waiting for transfers between devices, padded_2(): after = lax.ppermute(first, axis, down)  8.48 us
    ppermute x2, starting transfers between devices, padded_2(): before = lax.ppermute(last, axis, up)  8.01 us
    dot_general x18, matrix products, causal_conv(): jnp.dot(tap_rows, kernel[tap_t, tap_h], preferred_element_type=jnp.float32)  7.32 us
    all_to_all x1, starting transfers between devices, shards(): lax.all_to_all(latents, 'sect', split_axis=0, concat_axis=1, tiled=True)  4.23 us
    all_to_all x1, waiting for transfers between devices, shards(): lax.all_to_all(latents, 'sect', split_axis=0, concat_axis=1, tiled=True)  3.79 us
  transfers between devices with their start and end apart: 7, of which 7 were waited for; matrix products, arithmetic and copies ran while one was open for 0% of the time, Pallas kernels for 0%

commit v1 on v0

v1 whole, which is shorter than its diff:
```python
import functools

import jax
import jax.numpy as jnp
from jax import lax
from jax.experimental import pallas as pl
from jax.experimental.pallas import tpu as pltpu
from jax.sharding import PartitionSpec as P

GROUPS = 32
EPSILON = 1e-06
MESH = pl.DeviceIdType.MESH
F32 = jnp.float32
BF16 = jnp.bfloat16


def iota(shape, dim):
    return lax.broadcasted_iota(jnp.int32, shape, dim)


def pieces(row, first, rows=8):
    high = row.astype(BF16).astype(F32)
    rest = row - high
    mid = rest.astype(BF16).astype(F32)
    low = rest - mid
    width = row.shape[-1]
    ids = iota((rows, width), 0)
    out = jnp.zeros((rows, width), F32)
    for k, part in enumerate((high, mid, low)):
        out = jnp.where(ids == first + k, jnp.broadcast_to(part, (rows, width)), out)
    return out


def kernel(
    sizes,
    lat_ref,
    w1_ref,
    gain_ref,
    shift_ref,
    up_ref,
    out_ref,
    sendbuf,
    latbuf,
    w1_buf,
    lhs1,
    pre,
    gfull,
    gsum,
    gexp,
    stats,
    raw,
    mixed,
    lhs2,
    grid_out,
    up_sem,
    lat_send,
    lat_recv,
    st_send,
    st_recv,
):
    n_tm, n_tile, n_sect = sizes
    clips, blk, _, rows, cols, lat_ch = lat_ref.shape
    chans = w1_ref.shape[-1]
    out_ch = up_ref.shape[-1]
    group = chans // GROUPS
    span = blk * n_sect
    strip = blk * rows
    frames = 2 * span
    act_f = span + 2
    act_c = cols + 2
    cell = act_f * rows
    peers = n_tm * n_tile

    tm = lax.axis_index("tm")
    q = lax.axis_index("tile")
    sect = lax.axis_index("sect")
    me = tm * n_tile + q

    ups = []
    for a in range(3):
        copy = pltpu.make_async_copy(
            up_ref.at[a], raw.at[:, :, pl.ds(a * chans, chans), :], up_sem.at[a]
        )
        copy.start()
        ups.append(copy)

    def inside(dtm, dq):
        return (tm + dtm >= 0) & (tm + dtm < n_tm) & (q + dq >= 0) & (q + dq < n_tile)

    barrier = pltpu.get_barrier_semaphore()

    def peer_of(k):
        other = lax.rem(me + k, peers)
        return (other // n_tile, lax.rem(other, n_tile), sect)

    def greet(k, carry):
        pl.semaphore_signal(barrier, inc=1, device_id=peer_of(k), device_id_type=MESH)
        return carry

    for ds in range(1, n_sect):
        for dtm in range(2):
            for dq in (-1, 0, 1):

                @pl.when(inside(-dtm, dq))
                def _(dtm=dtm, dq=dq, ds=ds):
                    pl.semaphore_signal(
                        barrier,
                        inc=1,
                        device_id=(tm - dtm, q + dq, lax.rem(sect + n_sect - ds, n_sect)),
                        device_id_type=MESH,
                    )

    lax.fori_loop(1, peers, greet, 0)

    width = 128
    x = lat_ref[:, :, 0].astype(F32)
    placed = jnp.zeros((clips * strip, 3 * width), F32)
    for j in range(cols):
        col = x[:, :, :, j, :].reshape(clips * strip, lat_ch).astype(BF16)
        r = iota((lat_ch, 3 * width), 0)
        c = iota((lat_ch, 3 * width), 1)
        hit = (c == width + (j + 2) * lat_ch + r)
        if j >= cols - 2:
            hit = hit | (c == (j - cols + 2) * lat_ch + r)
        if j < 2:
            hit = hit | (c == 2 * width + (j + 2 + cols) * lat_ch + r)
        place = jnp.where(hit, 1.0, 0.0).astype(BF16)
        placed = placed + jnp.dot(col, place, preferred_element_type=F32)
    for pos in range(3):
        sendbuf[pos] = (
            placed[:, pos * width : (pos + 1) * width].astype(BF16).reshape(clips, strip, width)
        )

    targets = n_sect - 1
    steps_tm = jnp.where(tm + 1 < n_tm, 2, 1)
    steps_q = 1 + jnp.where(q > 0, 1, 0) + jnp.where(q + 1 < n_tile, 1, 0)
    pl.semaphore_wait(barrier, peers - 1 + targets * steps_tm * steps_q)

    def lat_copy(dtm, dq, ds, src_tm, src_q, src_sect):
        clip = lax.rem(src_sect + ds, n_sect)
        pos = 1 - dq
        slot = (1 - dtm) * n_sect + src_sect
        return pltpu.make_async_remote_copy(
            src_ref=sendbuf.at[pos, clip],
            dst_ref=latbuf.at[slot, pos],
            send_sem=lat_send.at[dtm, pos, ds],
            recv_sem=lat_recv.at[slot, pos],
            device_id=(src_tm + dtm, src_q + dq, clip),
            device_id_type=MESH,
        )

    moves = [
        (dtm, dq, ds)
        for ds in reversed(range(n_sect))
        for dq in (1, -1, 0)
        for dtm in (1, 0)
        if (dtm, dq, ds) != (0, 0, 0)
    ]
    for dtm, dq, ds in moves:

        @pl.when(inside(dtm, dq))
        def _(dtm=dtm, dq=dq, ds=ds):
            lat_copy(dtm, dq, ds, tm, q, sect).start()

    latbuf[n_sect + sect, 1] = sendbuf[1, sect]
    for dtm, dq, ds in moves:

        @pl.when(jnp.logical_not(inside(-dtm, -dq)))
        def _(dtm=dtm, dq=dq, ds=ds):
            slot = (1 - dtm) * n_sect + lax.rem(sect + n_sect - ds, n_sect)
            latbuf[slot, 1 - dq] = jnp.zeros((strip, width), BF16)

    w1_buf[...] = jnp.zeros(w1_buf.shape, BF16)
    for a in range(3):
        for b in range(3):
            for e in range(3):
                w1_buf[pl.ds(a * 256 + b * 64 + e * lat_ch, lat_ch), :] = w1_ref[a, b, e]

    r = iota((chans, chans), 0)
    c = iota((chans, chans), 1)
    gfull[...] = jnp.where(r // group == c // group, 1.0, 0.0).astype(BF16)
    r = iota((chans, 128), 0)
    c = iota((chans, 128), 1)
    gsum[...] = jnp.where((r >= c * group) & (r < (c + 1) * group), 1.0, 0.0).astype(BF16)
    r = iota((128, chans), 0)
    c = iota((128, chans), 1)
    gexp[...] = jnp.where((c >= r * group) & (c < (r + 1) * group), 1.0, 0.0).astype(BF16)

    step = 16

    def mix(k, carry):
        at = pl.ds(pl.multiple_of(k * step, step), step)
        taps = [[raw[b, e, at, :].astype(F32) for e in range(3)] for b in range(3)]
        sums = [
            taps[0],
            [taps[1][e] + taps[2][e] for e in range(3)],
            [taps[0][e] + taps[1][e] for e in range(3)],
            taps[2],
        ]
        for i, row in enumerate(sums):
            if i in (1, 2):
                mixed[i, 0, at, :] = row[0].astype(BF16)
                mixed[i, 3, at, :] = row[2].astype(BF16)
            mixed[i, 1, at, :] = (row[1] + row[2]).astype(BF16)
            mixed[i, 2, at, :] = (row[0] + row[1]).astype(BF16)
        return carry

    per = chans // step
    for a in range(2):
        ups[a].wait()
        lax.fori_loop(a * per, (a + 1) * per, mix, 0)

    for dtm, dq, ds in moves:

        @pl.when(inside(-dtm, -dq))
        def _(dtm=dtm, dq=dq, ds=ds):
            src = lax.rem(sect + n_sect - ds, n_sect)
            lat_copy(dtm, dq, ds, tm - dtm, q - dq, src).wait_recv()

    cells = (
        latbuf[:, 0].astype(F32) + latbuf[:, 1].astype(F32) + latbuf[:, 2].astype(F32)
    ).reshape(frames * rows, width)
    row_id = lax.rem(iota((frames * rows, width), 0), rows)
    lane = iota((frames * rows, width), 1)
    above = jnp.where(row_id == 0, 0.0, pltpu.roll(cells, 1, 0))
    below = jnp.where(row_id == rows - 1, 0.0, pltpu.roll(cells, frames * rows - 1, 0))
    for j in range(act_c):
        back = (width - j * lat_ch) % width
        half = (width + 64 - j * lat_ch) % width
        r0 = pltpu.roll(above, back, 1) if back else above
        r1 = pltpu.roll(cells, half, 1) if half else cells
        r2 = pltpu.roll(below, back, 1) if back else below
        both = jnp.where(lane < 64, r0, r1)
        for a in range(3):
            at = pl.ds(j * cell, cell)
            lhs1[at, a * 256 : a * 256 + 128] = both[a * rows : a * rows + cell].astype(BF16)
            lhs1[at, a * 256 + 128 : a * 256 + 256] = r2[a * rows : a * rows + cell].astype(BF16)
    pre[...] = jnp.dot(lhs1[...], w1_buf[...], preferred_element_type=F32)

    count = span * rows * cols
    own = [pl.ds(j * cell + 2 * rows, span * rows) for j in range(1, cols + 1)]
    total = jnp.zeros((1, chans), F32)
    for at in own:
        total = total + jnp.sum(pre[at, :], axis=0, keepdims=True)
    scaled = total * (1.0 / (count * group))
    parts = pieces(scaled, 0)
    local = jnp.sum(
        jnp.dot(parts.astype(BF16), gfull[...], preferred_element_type=F32), axis=0, keepdims=True
    )
    square = jnp.zeros((1, chans), F32)
    for at in own:
        off = pre[at, :] - local
        square = square + jnp.sum(off * off, axis=0, keepdims=True)
    both = parts + pieces(square, 3)
    sums = jnp.dot(both.astype(BF16), gsum[...], preferred_element_type=F32)
    ids = iota(sums.shape, 0)
    local_mean = jnp.sum(jnp.where(ids < 3, sums, 0.0), axis=0, keepdims=True)
    local_sq = jnp.sum(jnp.where(ids >= 3, sums, 0.0), axis=0, keepdims=True)
    stats[me] = jnp.concatenate([local_mean, local_sq], axis=0)

    def send_stats(k, carry):
        pltpu.make_async_remote_copy(
            src_ref=stats.at[me],
            dst_ref=stats.at[me],
            send_sem=st_send,
            recv_sem=st_recv,
            device_id=peer_of(k),
            device_id_type=MESH,
        ).start()
        return carry

    lax.fori_loop(1, peers, send_stats, 0)

    ups[2].wait()
    lax.fori_loop(2 * per, 3 * per, mix, 0)

    some = stats.at[pl.ds(0, peers - 1)]
    pltpu.make_async_copy(some, some, st_recv).wait()

    all_mean = jnp.zeros((1, 128), F32)
    for p in range(peers) if peers <= 16 else ():
        all_mean = all_mean + stats[p, 0:1, :]
    if peers > 16:
        all_mean = lax.fori_loop(0, peers, lambda p, t: t + stats[p, 0:1, :], all_mean)
    all_mean = all_mean * (1.0 / peers)

    def spread(p, acc):
        off = stats[p, 0:1, :] - all_mean
        return acc + stats[p, 1:2, :] + off * off * float(count * group)

    all_sq = jnp.zeros((1, 128), F32)
    if peers <= 16:
        for p in range(peers):
            all_sq = spread(p, all_sq)
    else:
        all_sq = lax.fori_loop(0, peers, spread, all_sq)
    inv = lax.rsqrt(all_sq * (1.0 / (peers * count * group)) + EPSILON)
    wide = jnp.dot(
        (pieces(all_mean, 0) + pieces(inv, 3)).astype(BF16), gexp[...], preferred_element_type=F32
    )
    ids = iota(wide.shape, 0)
    mean_c = jnp.sum(jnp.where(ids < 3, wide, 0.0), axis=0, keepdims=True)
    inv_c = jnp.sum(jnp.where(ids >= 3, wide, 0.0), axis=0, keepdims=True)
    scale_c = inv_c * gain_ref[...]
    shift_c = shift_ref[...]

    row_id = lax.rem(iota((cell, chans), 0), rows)
    early = iota((cell, chans), 0) < 2 * rows
    dead = early & (tm == 0)
    for j in range(act_c):
        y = (pre[pl.ds(j * cell, cell), :] - mean_c) * scale_c + shift_c
        act = y / (1.0 + jnp.exp(-y))
        gone = dead
        if j == 0:
            gone = gone | (q == 0)
        if j == act_c - 1:
            gone = gone | (q == n_tile - 1)
        act = jnp.where(gone, 0.0, act)
        above = jnp.where(row_id == 0, 0.0, pltpu.roll(act, 1, 0))
        below = jnp.where(row_id == rows - 1, 0.0, pltpu.roll(act, cell - 1, 0))
        for s, moved in enumerate((above, act, below)):
            for a in range(3):
                lhs2[s, pl.ds(j * span * rows, span * rows), a * chans : (a + 1) * chans] = moved[
                    a * rows : a * rows + span * rows
                ].astype(BF16)

    def weight(i, k):
        if i in (0, 3) and k in (0, 3):
            return raw[i - i // 3, k - k // 3]
        return mixed[i, k]

    many = cols * span * rows
    for ri in range(2):
        for cj in range(2):
            acc = jnp.zeros((many, out_ch), F32)
            for u in range(2):
                for v in range(2):
                    left = lhs2[ri + u, pl.ds((cj + v) * span * rows, many), :]
                    acc = acc + jnp.dot(
                        left, weight(2 * ri + u, 2 * cj + v), preferred_element_type=F32
                    )
            for j in range(cols):
                for t in range(span):
                    part = acc[(j * span + t) * rows : (j * span + t + 1) * rows]
                    first = t * 4 * rows * cols + ri * 2 * cols + 2 * j + cj
                    for h in range(out_ch // 128):
                        grid_out[h, pl.ds(first, rows, 4 * cols), :] = part[
                            :, h * 128 : (h + 1) * 128
                        ]
    for h in range(out_ch // 128):
        out_ref[0, :, 0, :, :, h * 128 : (h + 1) * 128] = (
            grid_out[h].reshape(span, 2 * rows, 2 * cols, 128).astype(BF16)
        )

    for dtm, dq, ds in moves:

        @pl.when(inside(dtm, dq))
        def _(dtm=dtm, dq=dq, ds=ds):
            lat_copy(dtm, dq, ds, tm, q, sect).wait_send()

    pltpu.make_async_copy(some, some, st_send).wait()


def shards(sizes, latents, in_weight, gn_gain, gn_shift, up_weight):
    n_tm, n_tile, n_sect = sizes
    clips, blk, _, rows, cols, lat_ch = latents.shape
    chans, out_ch = in_weight.shape[-1], up_weight.shape[-1]
    span = blk * n_sect
    cell = (span + 2) * rows
    act_c = cols + 2
    peers = n_tm * n_tile
    vmem = pl.BlockSpec(memory_space=pltpu.VMEM)
    return pl.pallas_call(
        functools.partial(kernel, sizes),
        out_shape=jax.ShapeDtypeStruct((1, span, 1, 2 * rows, 2 * cols, out_ch), BF16),
        in_specs=[vmem, vmem, vmem, vmem, pl.BlockSpec(memory_space=pltpu.HBM)],
        out_specs=vmem,
        scratch_shapes=[
            pltpu.VMEM((3, clips, blk * rows, 128), BF16),
            pltpu.VMEM((2 * n_sect, 3, blk * rows, 128), BF16),
            pltpu.VMEM((768, chans), BF16),
            pltpu.VMEM((act_c * cell, 768), BF16),
            pltpu.VMEM((act_c * cell, chans), F32),
            pltpu.VMEM((chans, chans), BF16),
            pltpu.VMEM((chans, 128), BF16),
            pltpu.VMEM((128, chans), BF16),
            pltpu.VMEM((peers, 2, 128), F32),
            pltpu.VMEM((3, 3, 3 * chans, out_ch), BF16),
            pltpu.VMEM((4, 4, 3 * chans, out_ch), BF16),
            pltpu.VMEM((3, act_c * span * rows, 3 * chans), BF16),
            pltpu.VMEM((out_ch // 128, span * 4 * rows * cols, 128), F32),
            pltpu.SemaphoreType.DMA((3,)),
            pltpu.SemaphoreType.DMA((2, 3, n_sect)),
            pltpu.SemaphoreType.DMA((2 * n_sect, 3)),
            pltpu.SemaphoreType.DMA,
            pltpu.SemaphoreType.DMA,
        ],
        compiler_params=pltpu.CompilerParams(
            collective_id=0, has_side_effects=True, vmem_limit_bytes=56 * 1024 * 1024
        ),
        cost_estimate=pl.CostEstimate(
            flops=2_500_000_000, bytes_accessed=8_000_000, transcendentals=300_000
        ),
    )(latents, in_weight, gn_gain.reshape(1, chans), gn_shift.reshape(1, chans), up_weight)


def solution(mesh):
    sizes = (mesh.shape["tm"], mesh.shape["tile"], mesh.shape["sect"])
    placed = (P(None, ("tm", "sect"), "tile", None, None, None), P(), P(), P(), P())
    return jax.shard_map(
        functools.partial(shards, sizes),
        mesh=mesh,
        in_specs=placed,
        out_specs=P("sect", "tm", "tile", None, None, None),
        check_vma=False,
    )
```

time: 120 us -> 19.5 us (0.16)
  blocking collectives: 62 us -> 0 us
  Pallas kernels: 0 us -> 17.7 us
  starting transfers between devices: 17.4 us -> 0 us
  local copies, waits for them, and re-layouts: 16.2 us -> 1.67 us
  waiting for transfers between devices: 14.5 us -> 0 us
  matrix products: 7.32 us -> 0 us
  other arithmetic: 1.74 us -> 0 us
    psum x2 -> x0, blocking collectives: 62 us -> none  [the longest x1 32.4 us: shards(): lax.psum(jnp.sum(grouped, axis=(1, 3)), ('tm', 'tile')) / cell_count]
    pallas_call x0 -> x1, Pallas kernels: none -> 17.7 us  [shards(): pl.pallas_call(functools.partial(kernel, sizes), out_shape=jax.ShapeDtype...]
    ppermute x6 -> x0, starting transfers between devices: 13.2 us -> none  [the longest x2 8.01 us: padded_2(): before = lax.ppermute(last, axis, up)]
    slice x16 -> x0, local copies, waits for them, and re-layouts: 12.4 us -> none  [the longest x11 11.5 us: causal_conv(): stacked[:, tap_t:tap_t + out_frames, tap_h:tap_h + out_rows]]
    ppermute x6 -> x0, waiting for transfers between devices: 10.7 us -> none  [the longest x2 8.48 us: padded_2(): after = lax.ppermute(first, axis, down)]
    dot_general x18 -> x0, matrix products: 7.32 us -> none  [causal_conv(): jnp.dot(tap_rows, kernel[tap_t, tap_h], preferred_element_type=jnp.float32)]
    all_to_all x1 -> x0, starting transfers between devices: 4.23 us -> none  [shards(): lax.all_to_all(latents, 'sect', split_axis=0, concat_axis=1, tiled=True)]
    all_to_all x1 -> x0, waiting for transfers between devices: 3.79 us -> none  [shards(): lax.all_to_all(latents, 'sect', split_axis=0, concat_axis=1, tiled=True)]
  transfers between devices with their start and end apart: 7 -> 0, of which waited for: 7 -> 0; matrix products, arithmetic and copies ran while one was open for 0% -> 0% of each run, Pallas kernels for 0% -> 0%
where the time goes in v1:
time: 19.5 us; the launch traced here: 19.4 us
  Pallas kernels  17.7 us (91%)
  local copies, waits for them, and re-layouts  1.67 us (9%)
    pallas_call x1, Pallas kernels, shards(): pl.pallas_call(functools.partial(kernel, sizes), out_shape=jax.ShapeDtype...  17.7 us
    unnamed x1, local copies, waits for them, and re-layouts  1.67 us

profile of v1, /device:TPU:0, one launch (start us, length us, event | category | flops | bytes accessed | tf_op | source)
XLA Modules:
  0.0 19.4 jit_solution(15100735108354356188)
XLA Ops:
  0.0 17.7 %shard_map.55 = bf16[1,4,1,16,8,256]{5,4,3,2,1,0:T(8,128)(2,1)} custom-call(bf16[2,2,1,8,4,16]{5,4,3,2,1,0:T(4,128)(2,1)} %lat_ref.1, bf16[3,3,3,16,512]{4,3,2,1,0:T(8,128)(2,1)} %w1_ref.1, f32[1,512]{1,0:T(1,128)} %bitcast.2, f32[1,512]{1,0:T(1,128)} %bitcast.3, bf16[3,3,3,512,256]{4,3,2,1,0:T(8,128)(2,1)} %up_ref.1), custom_call_target="tpu_custom_call" | custom-call | flops 2500000000 | bytes 8000000 | tf_op jit(solution)/shard_map/pallas_call | solution.py:373
  17.7 1.7 %copy.7 = bf16[1,4,1,16,8,256]{5,4,3,2,1,0:T(8,128)(2,1)} copy(bf16[1,4,1,16,8,256]{5,4,3,2,1,0:T(8,128)(2,1)} %shard_map.55) | data formatting | bytes 524288

commit v2 on v1

--- a/solution.py
+++ b/solution.py
@@ -33,12 +33,15 @@
 
 def kernel(
     sizes,
+    lat_hbm,
+    w1_hbm,
+    gain_hbm,
+    shift_hbm,
+    up_ref,
+    out_ref,
     lat_ref,
-    w1_ref,
     gain_ref,
     shift_ref,
-    up_ref,
-    out_ref,
     sendbuf,
     latbuf,
     w1_buf,
@@ -52,6 +55,7 @@
     mixed,
     lhs2,
     grid_out,
+    in_sem,
     up_sem,
     lat_send,
     lat_recv,
@@ -59,8 +63,8 @@
     st_recv,
 ):
     n_tm, n_tile, n_sect = sizes
-    clips, blk, _, rows, cols, lat_ch = lat_ref.shape
-    chans = w1_ref.shape[-1]
+    clips, blk, _, rows, cols, lat_ch = lat_hbm.shape
+    chans = w1_hbm.shape[-1]
     out_ch = up_ref.shape[-1]
     group = chans // GROUPS
     span = blk * n_sect
@@ -76,13 +80,13 @@
     sect = lax.axis_index("sect")
     me = tm * n_tile + q
 
-    ups = []
-    for a in range(3):
-        copy = pltpu.make_async_copy(
-            up_ref.at[a], raw.at[:, :, pl.ds(a * chans, chans), :], up_sem.at[a]
-        )
-        copy.start()
-        ups.append(copy)
+    loads = [
+        pltpu.make_async_copy(lat_hbm, lat_ref, in_sem.at[0]),
+        pltpu.make_async_copy(w1_hbm, w1_buf.at[:, pl.ds(0, 3), pl.ds(0, 3)], in_sem.at[1]),
+        pltpu.make_async_copy(gain_hbm, gain_ref, in_sem.at[2]),
+        pltpu.make_async_copy(shift_hbm, shift_ref, in_sem.at[3]),
+    ]
+    loads[0].start()
 
     def inside(dtm, dq):
         return (tm + dtm >= 0) & (tm + dtm < n_tm) & (q + dq >= 0) & (q + dq < n_tile)
@@ -93,10 +97,25 @@
         other = lax.rem(me + k, peers)
         return (other // n_tile, lax.rem(other, n_tile), sect)
 
-    def greet(k, carry):
+    far = sorted(range(n_tile), key=lambda d: -min(d, n_tile - d))
+    order = [d + c * n_tile for d in far for c in range(n_tm - 1, -1, -1) if d + c]
+
+    def each_peer(do):
+        if peers <= 16:
+            for k in order:
+                do(k)
+        else:
+
+            def body(k, carry):
+                do(k)
+                return carry
+
+            lax.fori_loop(1, peers, body, 0)
+
+    def greet(k):
         pl.semaphore_signal(barrier, inc=1, device_id=peer_of(k), device_id_type=MESH)
-        return carry
-
+
+    each_peer(greet)
     for ds in range(1, n_sect):
         for dtm in range(2):
             for dq in (-1, 0, 1):
@@ -110,9 +129,18 @@
                         device_id_type=MESH,
                     )
 
-    lax.fori_loop(1, peers, greet, 0)
+    for load in loads[1:]:
+        load.start()
+    ups = []
+    for a in range(3):
+        copy = pltpu.make_async_copy(
+            up_ref.at[a], raw.at[:, :, pl.ds(a * chans, chans), :], up_sem.at[a]
+        )
+        copy.start()
+        ups.append(copy)
 
     width = 128
+    loads[0].wait()
     x = lat_ref[:, :, 0].astype(F32)
     placed = jnp.zeros((clips * strip, 3 * width), F32)
     for j in range(cols):
@@ -170,11 +198,8 @@
             slot = (1 - dtm) * n_sect + lax.rem(sect + n_sect - ds, n_sect)
             latbuf[slot, 1 - dq] = jnp.zeros((strip, width), BF16)
 
-    w1_buf[...] = jnp.zeros(w1_buf.shape, BF16)
-    for a in range(3):
-        for b in range(3):
-            for e in range(3):
-                w1_buf[pl.ds(a * 256 + b * 64 + e * lat_ch, lat_ch), :] = w1_ref[a, b, e]
+    w1_buf[:, 3] = jnp.zeros((3, 4, lat_ch, chans), BF16)
+    w1_buf[:, 0:3, 3] = jnp.zeros((3, 3, lat_ch, chans), BF16)
 
     r = iota((chans, chans), 0)
     c = iota((chans, chans), 1)
@@ -235,7 +260,9 @@
             at = pl.ds(j * cell, cell)
             lhs1[at, a * 256 : a * 256 + 128] = both[a * rows : a * rows + cell].astype(BF16)
             lhs1[at, a * 256 + 128 : a * 256 + 256] = r2[a * rows : a * rows + cell].astype(BF16)
-    pre[...] = jnp.dot(lhs1[...], w1_buf[...], preferred_element_type=F32)
+    loads[1].wait()
+    w1 = w1_buf[...].reshape(768, chans)
+    pre[...] = jnp.dot(lhs1[...], w1, preferred_element_type=F32)
 
     count = span * rows * cols
     own = [pl.ds(j * cell + 2 * rows, span * rows) for j in range(1, cols + 1)]
@@ -258,7 +285,7 @@
     local_sq = jnp.sum(jnp.where(ids >= 3, sums, 0.0), axis=0, keepdims=True)
     stats[me] = jnp.concatenate([local_mean, local_sq], axis=0)
 
-    def send_stats(k, carry):
+    def send_stats(k):
         pltpu.make_async_remote_copy(
             src_ref=stats.at[me],
             dst_ref=stats.at[me],
@@ -267,9 +294,8 @@
             device_id=peer_of(k),
             device_id_type=MESH,
         ).start()
-        return carry
-
-    lax.fori_loop(1, peers, send_stats, 0)
+
+    each_peer(send_stats)
 
     ups[2].wait()
     lax.fori_loop(2 * per, 3 * per, mix, 0)
@@ -301,6 +327,8 @@
     ids = iota(wide.shape, 0)
     mean_c = jnp.sum(jnp.where(ids < 3, wide, 0.0), axis=0, keepdims=True)
     inv_c = jnp.sum(jnp.where(ids >= 3, wide, 0.0), axis=0, keepdims=True)
+    loads[2].wait()
+    loads[3].wait()
     scale_c = inv_c * gain_ref[...]
     shift_c = shift_ref[...]
 
@@ -373,12 +401,15 @@
     return pl.pallas_call(
         functools.partial(kernel, sizes),
         out_shape=jax.ShapeDtypeStruct((1, span, 1, 2 * rows, 2 * cols, out_ch), BF16),
-        in_specs=[vmem, vmem, vmem, vmem, pl.BlockSpec(memory_space=pltpu.HBM)],
+        in_specs=[pl.BlockSpec(memory_space=pltpu.HBM)] * 5,
         out_specs=vmem,
         scratch_shapes=[
+            pltpu.VMEM(latents.shape, BF16),
+            pltpu.VMEM((1, chans), F32),
+            pltpu.VMEM((1, chans), F32),
             pltpu.VMEM((3, clips, blk * rows, 128), BF16),
             pltpu.VMEM((2 * n_sect, 3, blk * rows, 128), BF16),
-            pltpu.VMEM((768, chans), BF16),
+            pltpu.VMEM((3, 4, 4, in_weight.shape[3], chans), BF16),
             pltpu.VMEM((act_c * cell, 768), BF16),
             pltpu.VMEM((act_c * cell, chans), F32),
             pltpu.VMEM((chans, chans), BF16),
@@ -389,6 +420,7 @@
             pltpu.VMEM((4, 4, 3 * chans, out_ch), BF16),
             pltpu.VMEM((3, act_c * span * rows, 3 * chans), BF16),
             pltpu.VMEM((out_ch // 128, span * 4 * rows * cols, 128), F32),
+            pltpu.SemaphoreType.DMA((4,)),
             pltpu.SemaphoreType.DMA((3,)),
             pltpu.SemaphoreType.DMA((2, 3, n_sect)),
             pltpu.SemaphoreType.DMA((2 * n_sect, 3)),

time: 19.5 us -> 18.4 us (0.944)
  Pallas kernels: 17.7 us -> 16.6 us
    pallas_call x1, Pallas kernels: 17.7 us -> 16.6 us  [shards(): pl.pallas_call(functools.partial(kernel, sizes), out_shape=jax.ShapeDtype...]
where the time goes in v2:
time: 18.4 us; the launch traced here: 18.3 us
  Pallas kernels  16.6 us (90%)
  local copies, waits for them, and re-layouts  1.67 us (9%)
    pallas_call x1, Pallas kernels, shards(): pl.pallas_call(functools.partial(kernel, sizes), out_shape=jax.ShapeDtype...  16.6 us
    unnamed x1, local copies, waits for them, and re-layouts  1.67 us

profile of v2, /device:TPU:0, one launch (start us, length us, event | category | flops | bytes accessed | tf_op | source)
XLA Modules:
  0.0 18.3 jit_solution(8321108861877841123)
XLA Ops:
  0.0 16.6 %shard_map.55 = bf16[1,4,1,16,8,256]{5,4,3,2,1,0:T(8,128)(2,1)} custom-call(bf16[2,2,1,8,4,16]{5,4,3,2,1,0:T(4,128)(2,1)} %lat_hbm.1, bf16[3,3,3,16,512]{4,3,2,1,0:T(8,128)(2,1)} %w1_hbm.1, f32[1,512]{1,0:T(1,128)} %bitcast.2, f32[1,512]{1,0:T(1,128)} %bitcast.3, bf16[3,3,3,512,256]{4,3,2,1,0:T(8,128)(2,1)} %up_ref.1), custom_call_target="tpu_custom_call" | custom-call | flops 2500000000 | bytes 8000000 | tf_op jit(solution)/shard_map/pallas_call | solution.py:401
  16.6 1.7 %copy.7 = bf16[1,4,1,16,8,256]{5,4,3,2,1,0:T(8,128)(2,1)} copy(bf16[1,4,1,16,8,256]{5,4,3,2,1,0:T(8,128)(2,1)} %shard_map.55) | data formatting | bytes 524288

commit v3 on v2

--- a/solution.py
+++ b/solution.py
@@ -400,7 +400,7 @@
     vmem = pl.BlockSpec(memory_space=pltpu.VMEM)
     return pl.pallas_call(
         functools.partial(kernel, sizes),
-        out_shape=jax.ShapeDtypeStruct((1, span, 1, 2 * rows, 2 * cols, out_ch), BF16),
+        out_shape=pltpu.VMEM((1, span, 1, 2 * rows, 2 * cols, out_ch), BF16),
         in_specs=[pl.BlockSpec(memory_space=pltpu.HBM)] * 5,
         out_specs=vmem,
         scratch_shapes=[

time: 18.4 us -> 16.8 us (0.913)
  local copies, waits for them, and re-layouts: 1.67 us -> 0.71 us
  Pallas kernels: 16.6 us -> 15.9 us
    unnamed x1, local copies, waits for them, and re-layouts: 1.67 us -> 0.71 us
    pallas_call x1, Pallas kernels: 16.6 us -> 15.9 us  [shards(): pl.pallas_call(functools.partial(kernel, sizes), out_shape=pltpu.VMEM((1,...]
where the time goes in v3:
time: 16.8 us; the launch traced here: 16.6 us
  Pallas kernels  15.9 us (95%)
  local copies, waits for them, and re-layouts  0.71 us (4%)
    pallas_call x1, Pallas kernels, shards(): pl.pallas_call(functools.partial(kernel, sizes), out_shape=pltpu.VMEM((1,...  15.9 us
    unnamed x1, local copies, waits for them, and re-layouts  0.71 us

profile of v3, /device:TPU:0, one launch (start us, length us, event | category | flops | bytes accessed | tf_op | source)
XLA Modules:
  0.0 16.6 jit_solution(5237065873068179147)
XLA Ops:
  0.0 15.9 %shard_map.55 = bf16[1,4,1,16,8,256]{5,4,3,2,1,0:T(8,128)(2,1)S(1)} custom-call(bf16[2,2,1,8,4,16]{5,4,3,2,1,0:T(4,128)(2,1)} %lat_hbm.1, bf16[3,3,3,16,512]{4,3,2,1,0:T(8,128)(2,1)} %w1_hbm.1, f32[1,512]{1,0:T(1,128)} %bitcast.2, f32[1,512]{1,0:T(1,128)} %bitcast.3, bf16[3,3,3,512,256]{4,3,2,1,0:T(8,128)(2,1)} %up_ref.1), custom_call_target="tpu_custom_call" | custom-call | flops 2500000000 | bytes 8000000 | tf_op jit(solution)/shard_map/pallas_call | solution.py:401
  15.9 0.7 %copy.7 = bf16[1,4,1,16,8,256]{5,4,3,2,1,0:T(8,128)(2,1)} copy(bf16[1,4,1,16,8,256]{5,4,3,2,1,0:T(8,128)(2,1)S(1)} %shard_map.55) | data formatting | bytes 524288

commit v4 on v3

--- a/solution.py
+++ b/solution.py
@@ -375,10 +375,13 @@
                         grid_out[h, pl.ds(first, rows, 4 * cols), :] = part[
                             :, h * 128 : (h + 1) * 128
                         ]
-    for h in range(out_ch // 128):
-        out_ref[0, :, 0, :, :, h * 128 : (h + 1) * 128] = (
-            grid_out[h].reshape(span, 2 * rows, 2 * cols, 128).astype(BF16)
-        )
+        for h in range(out_ch // 128):
+            for t in range(span):
+                for i in range(rows):
+                    first = ((t * rows + i) * 2 + ri) * 2 * cols
+                    out_ref[0, t, 0, 2 * i + ri, :, h * 128 : (h + 1) * 128] = grid_out[
+                        h, first : first + 2 * cols, :
+                    ].astype(BF16)
 
     for dtm, dq, ds in moves:
 

time: 16.8 us -> 16.8 us (level)
  no operation moved by 1% of the time
where the time goes in v4:
time: 16.8 us; the launch traced here: 16.6 us
  Pallas kernels  15.9 us (95%)
  local copies, waits for them, and re-layouts  0.71 us (4%)
    pallas_call x1, Pallas kernels, shards(): pl.pallas_call(functools.partial(kernel, sizes), out_shape=pltpu.VMEM((1,...  15.9 us
    unnamed x1, local copies, waits for them, and re-layouts  0.71 us

profile of v4, /device:TPU:0, one launch (start us, length us, event | category | flops | bytes accessed | tf_op | source)
XLA Modules:
  0.0 16.6 jit_solution(2024604646701665360)
XLA Ops:
  0.0 15.9 %shard_map.55 = bf16[1,4,1,16,8,256]{5,4,3,2,1,0:T(8,128)(2,1)S(1)} custom-call(bf16[2,2,1,8,4,16]{5,4,3,2,1,0:T(4,128)(2,1)} %lat_hbm.1, bf16[3,3,3,16,512]{4,3,2,1,0:T(8,128)(2,1)} %w1_hbm.1, f32[1,512]{1,0:T(1,128)} %bitcast.2, f32[1,512]{1,0:T(1,128)} %bitcast.3, bf16[3,3,3,512,256]{4,3,2,1,0:T(8,128)(2,1)} %up_ref.1), custom_call_target="tpu_custom_call" | custom-call | flops 2500000000 | bytes 8000000 | tf_op jit(solution)/shard_map/pallas_call | solution.py:404
  15.9 0.7 %copy.7 = bf16[1,4,1,16,8,256]{5,4,3,2,1,0:T(8,128)(2,1)} copy(bf16[1,4,1,16,8,256]{5,4,3,2,1,0:T(8,128)(2,1)S(1)} %shard_map.55) | data formatting | bytes 524288
